TPU v7x, 128 devices: a whole 4x4x4 slice. The times are simulated.
128 devices in a mesh: ctx: 8 (over x, z_lo), fsdp: 4 (over y), tp: 4 (over z_hi, core).
Axes of the slice: x: 4, y: 4, z: 4 (z_hi: 2, z_lo: 2; z = z_hi * 2 + z_lo), core: 2. Of those that a mesh axis runs over, the one named last changes fastest.
Arguments:
- base_ids: int32 [4, 2048], P('fsdp', 'ctx'), may hold values from 0 to 511
- embed_table: bfloat16 [512, 8192], P(None, 'tp'), may hold values from -6 to 6
- norm_gain: float32 [8192], replicated, may hold values from 0.1 to 1.9
- in_weight: bfloat16 [8192, 3, 4096], P('fsdp', None, 'tp'), may hold values from -0.0625 to 0.0625
- conv_taps: float32 [3, 3, 4096], P(None, None, 'tp'), may hold values from -3 to 3
- modal_poles: float32 [16, 4096], P(None, 'tp'), may hold values from 0.9 to 1, as said below
- residues: float32 [16, 4096], P(None, 'tp'), may hold values from -0.25 to 0.25
- skip_gain: float32 [4096], P('tp'), may hold values from -4 to 4
Outputs:
- mixed: bfloat16 [4, 2048, 4096], P('fsdp', 'ctx', 'tp')
Inputs may be any that keep to these rules, and one draw needn't show every extreme that they name: `modal_poles`: every pole lies strictly between 0 and 1.
All inputs are finite; a program needn't handle non-finite values.
Results may differ from a plain program's by a relative error of at most 0.008.
Values may be sent and summed in bfloat16 or wider, within the bound.
A program may use at most 256 MiB of HBM per device.

v0:
```python
import jax
import jax.numpy as jnp
from jax import lax
from jax.experimental import pallas as pl
from jax.experimental.pallas import tpu as pltpu
from jax.sharding import PartitionSpec as P

MESH = pl.DeviceIdType.MESH
F32 = jnp.float32
BF16 = jnp.bfloat16
norm_eps = 1e-06

CTX, FSDP, TP = 8, 4, 4
GROUP = CTX * FSDP
VOCAB = 512
ROWS = VOCAB // CTX
FEAT = 2048
CHAN = 1024
SLICE = CHAN // GROUP
STEPS = 256
POLES = 16
CHUNK = 256
CHUNKS = CHAN // CHUNK
SUB = 8


def iota(shape, dim):
    return lax.broadcasted_iota(jnp.int32, shape, dim)


OFFSETS = sorted(
    [(x, z, y) for x in range(4) for z in range(2) for y in range(4) if (x, z, y) != (0, 0, 0)],
    key=lambda o: -(min(o[0], 4 - o[0]) + o[1] + min(o[2], 4 - o[2])),
)


FAR_X = (2, 1, 3, 0)


def block_kernel(
    ids_ref, table_ref, gain_ref, weight_ref, taps_ref, poles_ref, res_ref, skip_ref, out_ref,
    weight_buf, own, rows, squares, send_buf, parts, all_ids, gain_buf, taps_buf, poles_buf, res_buf, skip_buf,
    params, kern, kmat, vmat, gmat, onehot, table, whole, raw, product, query, mixed,
    weight_sem, own_sem, small_sem, rows_sem, rows_send, sq_send, sq_recv, ids_send, ids_recv, part_send, part_recv,
    out_send, out_recv, ready,
):
    i = lax.axis_index("ctx")
    y = lax.axis_index("fsdp")
    t = lax.axis_index("tp")
    me = i * FSDP + y
    hi = lax.div(t, 2)
    flip = i + 1 - 2 * lax.rem(i, 2)
    turn = [lax.rem(lax.div(i, 2) + x, CHUNKS) for x in FAR_X]
    here = pl.ds(pl.multiple_of(i * 128, 128), 128)

    others = []
    for dx, dz, dy in OFFSETS:
        oi = lax.rem(lax.div(i, 2) + dx, 4) * 2 + lax.rem(lax.rem(i, 2) + dz, 2)
        oy = lax.rem(y + dy, FSDP)
        others.append((oi * FSDP + oy, (oi, oy, t)))

    barrier = pltpu.get_barrier_semaphore()

    def greet(device):
        pl.semaphore_signal(barrier, inc=1, device_id=device, device_id_type=MESH)

    for k in range(1, TP):
        greet((i, y, lax.rem(t + k, TP)))
    for core in range(2):
        greet((flip, y, (1 - hi) * 2 + core))
    for k in range(1, FSDP):
        greet((i, lax.rem(y + k, FSDP), t))
    columns_of = [(lax.rem(i + k, CTX), y, t) for k in range(1, CTX)]
    for device in columns_of:
        greet(device)

    def table_rows(block):
        return table_ref.at[pl.ds(pl.multiple_of(block * ROWS, ROWS), ROWS), :]

    def columns(step):
        return pl.ds(pl.multiple_of(turn[step] * CHUNK, CHUNK), CHUNK)

    def weight_copy(step):
        return pltpu.make_async_copy(weight_ref.at[:, :, columns(step)], weight_buf.at[step], weight_sem.at[step])

    own_copy = pltpu.make_async_copy(table_rows(i), own, own_sem)
    own_copy.start()
    small = [
        pltpu.make_async_copy(poles_ref, poles_buf, small_sem.at[0]),
        pltpu.make_async_copy(res_ref, res_buf, small_sem.at[1]),
        pltpu.make_async_copy(taps_ref, taps_buf, small_sem.at[2]),
        pltpu.make_async_copy(skip_ref, skip_buf, small_sem.at[3]),
        pltpu.make_async_copy(gain_ref, gain_buf, small_sem.at[4]),
    ]
    for copy in small:
        copy.start()
    for step in range(CHUNKS):
        weight_copy(step).start()

    pl.semaphore_wait(barrier, TP - 1 + 2 + FSDP - 1 + CTX - 1)

    piece_rows = ROWS // 4
    core = lax.rem(t, 2)
    sibling = hi * 2 + 1 - core
    home = lax.div(y, 2)

    def piece(ref, at):
        return ref.at[pl.ds(pl.multiple_of(at * piece_rows, piece_rows), piece_rows), :]

    def piece_to(source, at, device, slot):
        return pltpu.make_async_remote_copy(
            src_ref=piece(source, at), dst_ref=piece(rows, at), send_sem=rows_send.at[slot], recv_sem=rows_sem.at[at],
            device_id=device, device_id_type=MESH,
        )

    def arrived(at):
        return pltpu.make_async_copy(piece(rows, at), piece(rows, at), rows_sem.at[at])

    order = (0, 2, 1, 3)
    handed = [piece_to(table_rows(flip), at, (flip, y, (1 - hi) * 2 + at // 2), at) for at in order] + [
        piece_to(table_rows(i), at, (i, y, sibling), 4 + at) for at in order
    ]
    forward = [piece_to(rows, core * 2 + k, (i, y, sibling), k) for k in range(2)]

    @pl.when(t == y)
    def _():
        for copy in handed:
            copy.start()
        for at in range(4):
            pltpu.make_async_copy(piece(table_rows(i), at), piece(rows, at), rows_sem.at[at]).start()

    for device in columns_of:
        pl.semaphore_signal(ready, inc=1, device_id=device, device_id_type=MESH)

    own_copy.wait()
    mine = own[...].astype(F32)
    sums = jnp.sum(mine * mine, axis=1, keepdims=True)
    diagonal = iota((ROWS, 128), 0) == iota((ROWS, 128), 1)
    flat = jnp.sum(jnp.where(diagonal, sums, 0.0), axis=0, keepdims=True)
    squares[t] = jnp.broadcast_to(flat, (8, 128))

    def squares_to(k):
        return pltpu.make_async_remote_copy(
            src_ref=squares.at[t], dst_ref=squares.at[t], send_sem=sq_send.at[k], recv_sem=sq_recv.at[t],
            device_id=(i, y, lax.rem(t + k, TP)), device_id_type=MESH,
        )

    for k in range(1, TP):
        squares_to(k).start()

    for copy in small:
        copy.wait()
    stacked = jnp.concatenate(
        [poles_buf[:, here], res_buf[:, here]]
        + [taps_buf[s, n : n + 1, here] for s in range(3) for n in range(3)]
        + [skip_buf[:, here], jnp.zeros((128 - 2 * POLES - 10, 128), F32)],
        axis=0,
    )
    params[...] = stacked.T

    lag = iota((SUB, STEPS), 1).astype(F32)
    for g in range(SLICE // SUB):
        block = params[pl.ds(pl.multiple_of(y * SLICE + g * SUB, SUB), SUB), :]
        rates = jnp.log(block)
        total = jnp.zeros((SUB, STEPS), F32)
        for n in range(POLES):
            rate = rates[:, n : n + 1]
            lifted = block[:, POLES + n : POLES + n + 1] * jnp.exp(lag * rate)
            total = total + lifted
            at = pl.ds(n * SUB, SUB)
            gmat[g, at, :] = (lifted * block[:, n : n + 1]).astype(BF16)
            vmat[g, at, :] = jnp.exp((STEPS - 1 - lag) * rate).astype(BF16)
        kern[0, pl.ds(g * SUB, SUB), :] = total[:, :128]
        kern[1, pl.ds(g * SUB, SUB), :] = total[:, 128:]

    @pl.when(hi != home)
    def _():
        for k in range(2):
            arrived(core * 2 + k).wait()
            forward[k].start()

    def ids_to(other, device):
        return pltpu.make_async_remote_copy(
            src_ref=ids_ref, dst_ref=all_ids.at[y, pl.ds(i, 1), :], send_sem=ids_send.at[other],
            recv_sem=ids_recv.at[me], device_id=device, device_id_type=MESH,
        )

    pltpu.make_async_copy(ids_ref, all_ids.at[y, pl.ds(i, 1), :], ids_recv.at[me]).start()
    pl.semaphore_wait(ready, CTX - 1)
    for other, device in others:
        ids_to(other, device).start()

    for k in range(1, TP):
        source = lax.rem(t + k, TP)
        pltpu.make_async_copy(squares.at[source], squares.at[source], sq_recv.at[source]).wait()
    total = squares[0] + squares[1] + squares[2] + squares[3]
    scale = lax.rsqrt(total[0:1, :] * (1.0 / (FEAT * FSDP)) + norm_eps)
    scale = jnp.sum(jnp.where(diagonal, scale, 0.0), axis=1, keepdims=True)

    @pl.when(hi == home)
    def _():
        for k in range(2):
            arrived(core * 2 + k).wait()

    for k in range(2):
        arrived((1 - core) * 2 + k).wait()
    gain = gain_buf[:, pl.ds(pl.multiple_of(y * FEAT, FEAT), FEAT)]
    normed = (rows[...].astype(F32) * scale * gain).astype(BF16)

    lane_block = lax.div(iota((48, 128), 1), SLICE)

    def part_to(slot, device):
        return pltpu.make_async_remote_copy(
            src_ref=send_buf.at[slot], dst_ref=parts.at[me], send_sem=part_send.at[slot], recv_sem=part_recv.at[i],
            device_id=device, device_id_type=MESH,
        )

    mine_at = lax.rem(me, 8)

    def receivers(step):
        for dx, dz, dy in OFFSETS:
            if dx == FAR_X[step]:
                oz, oy = lax.rem(lax.rem(i, 2) + dz, 2), lax.rem(y + dy, FSDP)
                yield oz * FSDP + oy, (turn[step] * 2 + oz, oy, t)

    for step in range(CHUNKS):
        weight_copy(step).wait()
        dots = [jnp.dot(normed, weight_buf[step, stream], preferred_element_type=F32) for stream in range(3)]
        for half in range(CHUNK // 128):
            cols = [dot[:, half * 128 : half * 128 + 128] for dot in dots]
            for b in range(4):
                base = [pltpu.roll(c, (32 * (s - b)) % 128, 1) if (s - b) % 4 else c for s, c in enumerate(cols)]
                tail = jnp.concatenate(
                    [pltpu.roll(c[48:64], (32 * (3 - b)) % 128, 1) if (3 - b) % 4 else c[48:64] for c in cols], axis=0
                )
                piece = jnp.where(
                    lane_block == 0,
                    base[0][:48],
                    jnp.where(lane_block == 1, base[1][:48], jnp.where(lane_block == 2, base[2][:48], tail)),
                )
                send_buf[step * 8 + half * 4 + b] = piece.astype(BF16)
        for slot, device in receivers(step):
            part_to(step * 8 + slot, device).start()
        if FAR_X[step] == 0:
            pltpu.make_async_copy(send_buf.at[step * 8 + mine_at], parts.at[me], part_recv.at[i]).start()

    odd = [lax.rem(lax.div(iota((8, 128), 0), 2**bit), 2) == 1 for bit in range(3)]
    above = iota((128, 128), 1) >= iota((128, 128), 0)

    def fill(g, carry):
        block = pl.ds(pl.multiple_of(g * SUB, SUB), SUB)
        lags = [kern[half, block, :] for half in range(2)]
        bases = [[jnp.broadcast_to(x[k : k + 1], (8, 128)) for x in lags] for k in range(SUB)]
        for bit in range(3):
            bases = [[jnp.where(odd[bit], pltpu.roll(x, 2**bit, 1), x) for x in pair] for pair in bases]
        for k in range(SUB):
            shifted = [
                jnp.concatenate([pltpu.roll(x, 8 * m, 1) if m else x for m in range(16)], axis=0) for x in bases[k]
            ]
            kmat[g * SUB + k, :, pl.ds(0, 128)] = jnp.where(above, shifted[0], 0.0).astype(BF16)
            kmat[g * SUB + k, :, pl.ds(128, 128)] = jnp.where(above, shifted[1], shifted[0]).astype(BF16)
        return carry

    vocab_row = iota((VOCAB // 2, STEPS), 0)

    def hot(s, carry):
        for j in range(CTX):
            landed = all_ids.at[s, pl.ds(j, 1), :]
            pltpu.make_async_copy(ids_ref, landed, ids_recv.at[j * FSDP + s]).wait()
            row = all_ids[s, pl.ds(j, 1), :]
            low = jnp.where(row >= VOCAB // 2, row - VOCAB // 2, row)
            onehot[s * CTX + j] = jnp.where(vocab_row == low, 1.0, 0.0).astype(BF16)
        return carry

    lax.fori_loop(0, SLICE // SUB, fill, 0)
    lax.fori_loop(0, FSDP, hot, 0)

    block16 = lax.div(iota((16, 128), 1), SLICE)
    for step in range(CHUNKS):
        pair = lax.rem(lax.div(i, 2) + 4 - FAR_X[step], CHUNKS)
        for z in range(2):
            four = parts.at[pl.ds((pair * 2 + z) * 4, 4)]
            pltpu.make_async_copy(four, four, part_recv.at[pair * 2 + z]).wait()
            a = parts[(pair * 2 + z) * 4].astype(F32)
            for k in range(1, 4):
                a = a + parts[(pair * 2 + z) * 4 + k].astype(F32)
            tail = [pltpu.roll(a[16 * s : 16 * s + 16], SLICE * (s + 1), 1) for s in range(3)]
            whole[pl.ds(z * ROWS, 48), :] = a
            whole[pl.ds(z * ROWS + 48, 16), :] = jnp.where(
                block16 == 0, tail[0], jnp.where(block16 == 1, tail[1], tail[2])
            )
        to = pl.ds(pl.multiple_of(lax.div(pair, 2) * (3 * SLICE), 3 * SLICE), 3 * SLICE)
        cols = pl.ds(pl.multiple_of(lax.rem(pair, 2) * 128, 128), 128)
        table[to, cols] = whole[...].T[: 3 * SLICE].astype(BF16)

    def gather(s, carry):
        for j in range(CTX):
            at = s * CTX + j
            both = jnp.dot(table[...], onehot[at], preferred_element_type=F32)
            upper = all_ids[s, pl.ds(j, 1), :] >= VOCAB // 2
            for half in range(2):
                cols = slice(half * 128, half * 128 + 128)
                raw[half, at] = jnp.where(upper[:, cols], both[3 * SLICE :, cols], both[: 3 * SLICE, cols])
        return carry

    lax.fori_loop(0, FSDP, gather, 0)

    lane = iota((SUB, 128), 1)

    def featurize(g):
        block = params[pl.ds(pl.multiple_of(y * SLICE + g * SUB, SUB), SUB), :]
        taps = [
            [
                jnp.broadcast_to(block[:, 2 * POLES + 3 * s + n : 2 * POLES + 3 * s + n + 1], (SUB, 128))
                for n in range(3)
            ]
            for s in range(3)
        ]
        for at in range(GROUP):
            if at % CTX == 0:
                before = [[jnp.zeros((SUB, 128), F32)] * 2] * 3
            for half in range(2):
                done = []
                for s in range(3):
                    now = raw[half, at, pl.ds(s * SLICE + g * SUB, SUB), :]
                    moved = [pltpu.roll(now, n, 1) for n in (1, 2)]
                    total = taps[s][0] * now
                    for n in (1, 2):
                        total = total + taps[s][n] * jnp.where(lane < n, before[s][n - 1], moved[n - 1])
                    before = before[:s] + [moved] + before[s + 1 :]
                    done.append(total)
                to = pl.ds(at * SUB, SUB)
                query[g][half, to, :] = done[0]
                product[g][half, to, :] = done[1] * done[2]

    same = lax.div(iota((SUB * GROUP, 128), 0), GROUP) == lax.rem(iota((SUB * GROUP, 128), 1), SUB)
    chunk = lax.rem(iota((SUB * GROUP, 128), 0), CTX)
    diagonal128 = iota((128, 128), 0) == iota((128, 128), 1)

    def convolve(g):
        block = params[pl.ds(pl.multiple_of(y * SLICE + g * SUB, SUB), SUB), :]
        decay = jnp.concatenate(
            [jnp.broadcast_to(block[:, n : n + 1], (SUB, 128)) for n in range(POLES)], axis=0
        )
        decay = jnp.sum(jnp.where(diagonal128, decay, 0.0), axis=0, keepdims=True)
        for _ in range(8):
            decay = decay * decay
        halves = [
            [product[g][half, pl.ds(k, GROUP, stride=SUB), :].astype(BF16) for half in range(2)] for k in range(SUB)
        ]
        inputs = jnp.concatenate([jnp.concatenate(x, axis=1) for x in halves], axis=0)
        states = lax.dot_general(inputs, vmat[g], (((1,), (1,)), ((), ())), preferred_element_type=F32)
        inner = []
        for k in range(SUB):
            both = jnp.dot(jnp.concatenate(halves[k], axis=0), kmat[g * SUB + k], preferred_element_type=F32)
            inner.append([both[:GROUP, :128], both[:GROUP, 128:] + both[GROUP:, :128]])
        states = jnp.where(same, states, 0.0)
        states = jnp.where(chunk < 1, 0.0, pltpu.roll(states, 1, 0))
        for by in (1, 2, 4):
            states = states + decay * jnp.where(chunk < by, 0.0, pltpu.roll(states, by, 0))
            decay = decay * decay
        carried = jnp.dot(states.astype(BF16), gmat[g], preferred_element_type=F32)
        for k in range(SUB):
            for half in range(2):
                mixed[g][half, pl.ds(k, GROUP, stride=SUB), :] = (
                    inner[k][half] + carried[k * GROUP : (k + 1) * GROUP, half * 128 : half * 128 + 128]
                )

    mine_params = params[pl.ds(pl.multiple_of(y * SLICE, SLICE), SLICE), :]
    skip = jnp.broadcast_to(mine_params[:, 2 * POLES + 9 : 2 * POLES + 10], (SLICE, 128))
    pieces = onehot

    def share(part):
        return pl.ds(part * 2 * SUB, 2 * SUB)

    def out_to(part, other, device):
        return pltpu.make_async_remote_copy(
            src_ref=pieces.at[other, share(part), :], dst_ref=out_ref.at[me, share(part), :],
            send_sem=out_send.at[part, other], recv_sem=out_recv, device_id=device, device_id_type=MESH,
        )

    def gate(part, other):
        s = lax.rem(other, FSDP)
        j = lax.div(other, FSDP)
        at = pl.ds(pl.multiple_of((s * CTX + j) * SUB, SUB), SUB)
        for half in range(2):
            q, u, c = [
                jnp.concatenate([x[2 * part + g][half, at, :] for g in range(2)], axis=0)
                for x in (query, product, mixed)
            ]
            gated = q * (c + skip[part * 2 * SUB : (part + 1) * 2 * SUB] * u)
            pieces[other, share(part), pl.ds(half * 128, 128)] = gated.astype(BF16)

    for part in range(2):
        featurize(2 * part)
        featurize(2 * part + 1)
        convolve(2 * part)
        convolve(2 * part + 1)
        for other, device in others:
            gate(part, other)
            out_to(part, other, device).start()
        gate(part, me)
        pltpu.make_async_copy(pieces.at[me, share(part), :], out_ref.at[me, share(part), :], out_recv).start()

    for k in range(1, TP):
        squares_to(k).wait_send()

    @pl.when(t == y)
    def _():
        for copy in handed:
            copy.wait_send()

    @pl.when(hi != home)
    def _():
        for copy in forward:
            copy.wait_send()

    for step in range(CHUNKS):
        for slot, device in receivers(step):
            part_to(step * 8 + slot, device).wait_send()

    for other, device in others:
        ids_to(other, device).wait_send()
        for part in range(2):
            out_to(part, other, device).wait_send()

    pltpu.make_async_copy(out_ref, out_ref, out_recv).wait()


def block(*args):
    hbm = pl.BlockSpec(memory_space=pltpu.HBM)
    dma = pltpu.SemaphoreType.DMA
    groups = SLICE // SUB
    return pl.pallas_call(
        block_kernel,
        out_shape=jax.ShapeDtypeStruct((GROUP, SLICE, STEPS), BF16),
        in_specs=[hbm] * 8,
        out_specs=hbm,
        scratch_shapes=[
            pltpu.VMEM((CHUNKS, 3, FEAT, CHUNK), BF16),
            pltpu.VMEM((ROWS, FEAT), BF16),
            pltpu.VMEM((ROWS, FEAT), BF16),
            pltpu.VMEM((TP, 8, 128), F32),
            pltpu.VMEM((GROUP, 48, 128), BF16),
            pltpu.VMEM((GROUP, 48, 128), BF16),
            pltpu.VMEM((FSDP, CTX, STEPS), jnp.int32),
            pltpu.VMEM((1, FEAT * FSDP), F32),
            pltpu.VMEM((3, 3, CHAN), F32),
            pltpu.VMEM((POLES, CHAN), F32),
            pltpu.VMEM((POLES, CHAN), F32),
            pltpu.VMEM((1, CHAN), F32),
            pltpu.VMEM((128, 128), F32),
            pltpu.VMEM((2, SLICE, 128), F32),
            pltpu.VMEM((SLICE, STEPS // 2, STEPS), BF16),
            pltpu.VMEM((groups, POLES * SUB, STEPS), BF16),
            pltpu.VMEM((groups, POLES * SUB, STEPS), BF16),
            pltpu.VMEM((GROUP, VOCAB // 2, STEPS), BF16),
            pltpu.VMEM((6 * SLICE, VOCAB // 2), BF16),
            pltpu.VMEM((2 * ROWS, 128), F32),
            pltpu.VMEM((2, GROUP, 3 * SLICE, 128), F32),
            [pltpu.VMEM((2, GROUP * SUB, 128), F32) for _ in range(groups)],
            [pltpu.VMEM((2, GROUP * SUB, 128), F32) for _ in range(groups)],
            [pltpu.VMEM((2, GROUP * SUB, 128), F32) for _ in range(groups)],
            dma((CHUNKS,)),
            dma,
            dma((5,)),
            dma((4,)),
            dma((8,)),
            dma((TP,)),
            dma((TP,)),
            dma((GROUP,)),
            dma((GROUP,)),
            dma((GROUP,)),
            dma((CTX,)),
            dma((2, GROUP)),
            dma,
            pltpu.SemaphoreType.REGULAR,
        ],
        compiler_params=pltpu.CompilerParams(
            collective_id=0, has_side_effects=True, vmem_limit_bytes=56 * 2**20
        ),
        name="hyena_block",
    )(*args)


def shards(
    base_ids, embed_table, norm_gain, in_weight, conv_taps, modal_poles, residues, skip_gain
):
    landed = block(
        base_ids, embed_table, norm_gain.reshape(1, -1), jnp.transpose(in_weight, (1, 0, 2)),
        conv_taps, modal_poles, residues, skip_gain.reshape(1, -1),
    )
    return landed.reshape(CHAN, STEPS).T[None]


def solution(mesh):
    in_specs = (
        P("fsdp", "ctx"),
        P(None, "tp"),
        P(),
        P("fsdp", None, "tp"),
        P(None, None, "tp"),
        P(None, "tp"),
        P(None, "tp"),
        P("tp"),
    )
    out_specs = P("fsdp", "ctx", "tp")
    return jax.shard_map(shards, mesh=mesh, in_specs=in_specs, out_specs=out_specs, check_vma=False)
```

profile of v0, /device:TPU:1, one launch (start us, length us, event | category | flops | bytes accessed | tf_op | source)
XLA Modules:
  0.0 37.9 jit_solution(16017354116689237450)
XLA Ops:
  0.0 35.9 %hyena_block.1 = bf16[32,32,256]{2,1,0:T(8,128)(2,1)} custom-call(s32[1,256]{1,0:T(1,128)} %ids_ref.1, bf16[512,2048]{1,0:T(8,128)(2,1)} %table_ref.1, f32[1,8192]{1,0:T(1,128)} %bitcast.9, bf16[3,2048,1024]{2,1,0:T(8,128)(2,1)} %bitcast.7, f32[3,3,1024]{2,1,0:T(4,128)} %taps_ref.1, f32[16,1024]{1,0:T(8,128)} %poles_ref.1, f32[16,1024]{1,0:T(8,128)} %res_ref.1, ...), custom_call_target="tpu_custom_call" | custom-call | tf_op jit(solution)/shard_map/hyena_block/pallas_call | solution.py:434
  35.9 2.0 %copy.9 = bf16[1024,256]{0,1:T(8,128)(2,1)} copy(bf16[1024,256]{1,0:T(8,128)(2,1)} %bitcast.8) | data formatting | bytes 1048576 | tf_op jit(solution)/shard_map/reshape | solution.py:493
where the time goes:
time: 38.2 us; the launch traced here: 37.9 us
  Pallas kernels  35.9 us (94%)
  local copies, waits for them, and re-layouts  2.04 us (5%)
    pallas_call x1, Pallas kernels, block(): pl.pallas_call(block_kernel, out_shape=jax.ShapeDtypeStruct((GROUP, SLICE...  35.9 us
    reshape x1, local copies, waits for them, and re-layouts, shards(): return landed.reshape(CHAN, STEPS).T[None]  2.04 us

commit v1 on v0

--- a/solution.py
+++ b/solution.py
@@ -40,7 +40,7 @@
 def block_kernel(
     ids_ref, table_ref, gain_ref, weight_ref, taps_ref, poles_ref, res_ref, skip_ref, out_ref,
     weight_buf, own, rows, squares, send_buf, parts, all_ids, gain_buf, taps_buf, poles_buf, res_buf, skip_buf,
-    params, kern, kmat, vmat, gmat, onehot, table, whole, raw, product, query, mixed,
+    params, decays, kern, kmat, vmat, gmat, onehot, table, whole, raw, product, query, mixed,
     weight_sem, own_sem, small_sem, rows_sem, rows_send, sq_send, sq_recv, ids_send, ids_recv, part_send, part_recv,
     out_send, out_recv, ready,
 ):
@@ -223,9 +223,15 @@
                 oz, oy = lax.rem(lax.rem(i, 2) + dz, 2), lax.rem(y + dy, FSDP)
                 yield oz * FSDP + oy, (turn[step] * 2 + oz, oy, t)
 
+    def multiply(step):
+        weight_copy(step).wait()
+        return [jnp.dot(normed, weight_buf[step, stream], preferred_element_type=F32) for stream in range(3)]
+
+    following = multiply(0)
     for step in range(CHUNKS):
-        weight_copy(step).wait()
-        dots = [jnp.dot(normed, weight_buf[step, stream], preferred_element_type=F32) for stream in range(3)]
+        dots = following
+        if step + 1 < CHUNKS:
+            following = multiply(step + 1)
         for half in range(CHUNK // 128):
             cols = [dot[:, half * 128 : half * 128 + 128] for dot in dots]
             for b in range(4):
@@ -273,6 +279,17 @@
         return carry
 
     lax.fori_loop(0, SLICE // SUB, fill, 0)
+    diagonal128 = iota((128, 128), 0) == iota((128, 128), 1)
+    for g in range(SLICE // SUB):
+        block = params[pl.ds(pl.multiple_of(y * SLICE + g * SUB, SUB), SUB), :]
+        decay = jnp.concatenate(
+            [jnp.broadcast_to(block[:, n : n + 1], (SUB, 128)) for n in range(POLES)], axis=0
+        )
+        decay = jnp.sum(jnp.where(diagonal128, decay, 0.0), axis=0, keepdims=True)
+        for _ in range(8):
+            decay = decay * decay
+        decays[g] = jnp.broadcast_to(decay, (8, 128))
+
     lax.fori_loop(0, FSDP, hot, 0)
 
     block16 = lax.div(iota((16, 128), 1), SLICE)
@@ -333,18 +350,11 @@
                 query[g][half, to, :] = done[0]
                 product[g][half, to, :] = done[1] * done[2]
 
-    same = lax.div(iota((SUB * GROUP, 128), 0), GROUP) == lax.rem(iota((SUB * GROUP, 128), 1), SUB)
-    chunk = lax.rem(iota((SUB * GROUP, 128), 0), CTX)
-    diagonal128 = iota((128, 128), 0) == iota((128, 128), 1)
+    channel = lax.rem(iota((GROUP, 128), 1), SUB)
+    chunk = lax.rem(iota((GROUP, 128), 0), CTX)
 
     def convolve(g):
-        block = params[pl.ds(pl.multiple_of(y * SLICE + g * SUB, SUB), SUB), :]
-        decay = jnp.concatenate(
-            [jnp.broadcast_to(block[:, n : n + 1], (SUB, 128)) for n in range(POLES)], axis=0
-        )
-        decay = jnp.sum(jnp.where(diagonal128, decay, 0.0), axis=0, keepdims=True)
-        for _ in range(8):
-            decay = decay * decay
+        decay = decays[g, 0:1, :]
         halves = [
             [product[g][half, pl.ds(k, GROUP, stride=SUB), :].astype(BF16) for half in range(2)] for k in range(SUB)
         ]
@@ -354,11 +364,15 @@
         for k in range(SUB):
             both = jnp.dot(jnp.concatenate(halves[k], axis=0), kmat[g * SUB + k], preferred_element_type=F32)
             inner.append([both[:GROUP, :128], both[:GROUP, 128:] + both[GROUP:, :128]])
-        states = jnp.where(same, states, 0.0)
+        stacked = states[:GROUP]
+        for k in range(1, SUB):
+            stacked = jnp.where(channel == k, states[k * GROUP : (k + 1) * GROUP], stacked)
+        states = stacked
         states = jnp.where(chunk < 1, 0.0, pltpu.roll(states, 1, 0))
         for by in (1, 2, 4):
             states = states + decay * jnp.where(chunk < by, 0.0, pltpu.roll(states, by, 0))
             decay = decay * decay
+        states = jnp.concatenate([jnp.where(channel == k, states, 0.0) for k in range(SUB)], axis=0)
         carried = jnp.dot(states.astype(BF16), gmat[g], preferred_element_type=F32)
         for k in range(SUB):
             for half in range(2):
@@ -450,6 +464,7 @@
             pltpu.VMEM((POLES, CHAN), F32),
             pltpu.VMEM((1, CHAN), F32),
             pltpu.VMEM((128, 128), F32),
+            pltpu.VMEM((groups, 8, 128), F32),
             pltpu.VMEM((2, SLICE, 128), F32),
             pltpu.VMEM((SLICE, STEPS // 2, STEPS), BF16),
             pltpu.VMEM((groups, POLES * SUB, STEPS), BF16),

time: 38.2 us -> 38.3 us (level)
  no operation moved by 1% of the time
where the time goes in v1:
time: 38.3 us; the launch traced here: 38.2 us
  Pallas kernels  36.1 us (94%)
  local copies, waits for them, and re-layouts  2.04 us (5%)
    pallas_call x1, Pallas kernels, block(): pl.pallas_call(block_kernel, out_shape=jax.ShapeDtypeStruct((GROUP, SLICE...  36.1 us
    reshape x1, local copies, waits for them, and re-layouts, shards(): return landed.reshape(CHAN, STEPS).T[None]  2.04 us

profile of v1, /device:TPU:1, one launch (start us, length us, event | category | flops | bytes accessed | tf_op | source)
XLA Modules:
  0.0 38.2 jit_solution(10060766409323960458)
XLA Ops:
  0.0 36.1 %hyena_block.1 = bf16[32,32,256]{2,1,0:T(8,128)(2,1)} custom-call(s32[1,256]{1,0:T(1,128)} %ids_ref.1, bf16[512,2048]{1,0:T(8,128)(2,1)} %table_ref.1, f32[1,8192]{1,0:T(1,128)} %bitcast.9, bf16[3,2048,1024]{2,1,0:T(8,128)(2,1)} %bitcast.7, f32[3,3,1024]{2,1,0:T(4,128)} %taps_ref.1, f32[16,1024]{1,0:T(8,128)} %poles_ref.1, f32[16,1024]{1,0:T(8,128)} %res_ref.1, ...), custom_call_target="tpu_custom_call" | custom-call | tf_op jit(solution)/shard_map/hyena_block/pallas_call | solution.py:448
  36.1 2.0 %copy.9 = bf16[1024,256]{0,1:T(8,128)(2,1)} copy(bf16[1024,256]{1,0:T(8,128)(2,1)} %bitcast.8) | data formatting | bytes 1048576 | tf_op jit(solution)/shard_map/reshape | solution.py:508

commit v2 on v1

--- a/solution.py
+++ b/solution.py
@@ -223,15 +223,9 @@
                 oz, oy = lax.rem(lax.rem(i, 2) + dz, 2), lax.rem(y + dy, FSDP)
                 yield oz * FSDP + oy, (turn[step] * 2 + oz, oy, t)
 
-    def multiply(step):
+    for step in range(CHUNKS):
         weight_copy(step).wait()
-        return [jnp.dot(normed, weight_buf[step, stream], preferred_element_type=F32) for stream in range(3)]
-
-    following = multiply(0)
-    for step in range(CHUNKS):
-        dots = following
-        if step + 1 < CHUNKS:
-            following = multiply(step + 1)
+        dots = [jnp.dot(normed, weight_buf[step, stream], preferred_element_type=F32) for stream in range(3)]
         for half in range(CHUNK // 128):
             cols = [dot[:, half * 128 : half * 128 + 128] for dot in dots]
             for b in range(4):

time: 38.3 us -> 38.1 us (level)
  no operation moved by 1% of the time
where the time goes in v2:
time: 38.1 us; the launch traced here: 37.9 us
  Pallas kernels  35.8 us (94%)
  local copies, waits for them, and re-layouts  2.04 us (5%)
    pallas_call x1, Pallas kernels, block(): pl.pallas_call(block_kernel, out_shape=jax.ShapeDtypeStruct((GROUP, SLICE...  35.8 us
    reshape x1, local copies, waits for them, and re-layouts, shards(): return landed.reshape(CHAN, STEPS).T[None]  2.04 us

profile of v2, /device:TPU:1, one launch (start us, length us, event | category | flops | bytes accessed | tf_op | source)
XLA Modules:
  0.0 37.9 jit_solution(9025037805342298243)
XLA Ops:
  0.0 35.8 %hyena_block.1 = bf16[32,32,256]{2,1,0:T(8,128)(2,1)} custom-call(s32[1,256]{1,0:T(1,128)} %ids_ref.1, bf16[512,2048]{1,0:T(8,128)(2,1)} %table_ref.1, f32[1,8192]{1,0:T(1,128)} %bitcast.9, bf16[3,2048,1024]{2,1,0:T(8,128)(2,1)} %bitcast.7, f32[3,3,1024]{2,1,0:T(4,128)} %taps_ref.1, f32[16,1024]{1,0:T(8,128)} %poles_ref.1, f32[16,1024]{1,0:T(8,128)} %res_ref.1, ...), custom_call_target="tpu_custom_call" | custom-call | tf_op jit(solution)/shard_map/hyena_block/pallas_call | solution.py:442
  35.8 2.0 %copy.9 = bf16[1024,256]{0,1:T(8,128)(2,1)} copy(bf16[1024,256]{1,0:T(8,128)(2,1)} %bitcast.8) | data formatting | bytes 1048576 | tf_op jit(solution)/shard_map/reshape | solution.py:502

commit v3 on v2

--- a/solution.py
+++ b/solution.py
@@ -211,7 +211,7 @@
 
     def part_to(slot, device):
         return pltpu.make_async_remote_copy(
-            src_ref=send_buf.at[slot], dst_ref=parts.at[me], send_sem=part_send.at[slot], recv_sem=part_recv.at[i],
+            src_ref=send_buf.at[slot], dst_ref=parts.at[me], send_sem=part_send, recv_sem=part_recv.at[i],
             device_id=device, device_id_type=MESH,
         )
 
@@ -285,6 +285,22 @@
         decays[g] = jnp.broadcast_to(decay, (8, 128))
 
     lax.fori_loop(0, FSDP, hot, 0)
+
+    for k in range(1, TP):
+        squares_to(k).wait_send()
+
+    @pl.when(t == y)
+    def _():
+        for copy in handed:
+            copy.wait_send()
+
+    @pl.when(hi != home)
+    def _():
+        for copy in forward:
+            copy.wait_send()
+
+    for other, device in others:
+        ids_to(other, device).wait_send()
 
     block16 = lax.div(iota((16, 128), 1), SLICE)
     for step in range(CHUNKS):
@@ -384,7 +400,7 @@
     def out_to(part, other, device):
         return pltpu.make_async_remote_copy(
             src_ref=pieces.at[other, share(part), :], dst_ref=out_ref.at[me, share(part), :],
-            send_sem=out_send.at[part, other], recv_sem=out_recv, device_id=device, device_id_type=MESH,
+            send_sem=out_send.at[part], recv_sem=out_recv, device_id=device, device_id_type=MESH,
         )
 
     def gate(part, other):
@@ -410,28 +426,11 @@
         gate(part, me)
         pltpu.make_async_copy(pieces.at[me, share(part), :], out_ref.at[me, share(part), :], out_recv).start()
 
-    for k in range(1, TP):
-        squares_to(k).wait_send()
-
-    @pl.when(t == y)
-    def _():
-        for copy in handed:
-            copy.wait_send()
-
-    @pl.when(hi != home)
-    def _():
-        for copy in forward:
-            copy.wait_send()
-
-    for step in range(CHUNKS):
-        for slot, device in receivers(step):
-            part_to(step * 8 + slot, device).wait_send()
-
-    for other, device in others:
-        ids_to(other, device).wait_send()
-        for part in range(2):
-            out_to(part, other, device).wait_send()
-
+    sent = send_buf.at[pl.ds(0, GROUP - 1)]
+    pltpu.make_async_copy(sent, sent, part_send).wait()
+    for part in range(2):
+        sent = pieces.at[pl.ds(0, GROUP - 1), share(part), :]
+        pltpu.make_async_copy(sent, sent, out_send.at[part]).wait()
     pltpu.make_async_copy(out_ref, out_ref, out_recv).wait()
 
 
@@ -479,9 +478,9 @@
             dma((TP,)),
             dma((GROUP,)),
             dma((GROUP,)),
-            dma((GROUP,)),
+            dma,
             dma((CTX,)),
-            dma((2, GROUP)),
+            dma((2,)),
             dma,
             pltpu.SemaphoreType.REGULAR,
         ],

time: 38.1 us -> 37.3 us (0.979)
  Pallas kernels: 35.8 us -> 35 us
    pallas_call x1, Pallas kernels: 35.8 us -> 35 us  [block(): pl.pallas_call(block_kernel, out_shape=jax.ShapeDtypeStruct((GROUP, SLICE...]
where the time goes in v3:
time: 37.3 us; the launch traced here: 37 us
  Pallas kernels  35 us (94%)
  local copies, waits for them, and re-layouts  2.04 us (5%)
    pallas_call x1, Pallas kernels, block(): pl.pallas_call(block_kernel, out_shape=jax.ShapeDtypeStruct((GROUP, SLICE...  35 us
    reshape x1, local copies, waits for them, and re-layouts, shards(): return landed.reshape(CHAN, STEPS).T[None]  2.04 us

profile of v3, /device:TPU:1, one launch (start us, length us, event | category | flops | bytes accessed | tf_op | source)
XLA Modules:
  0.0 37.0 jit_solution(6359168989988346844)
XLA Ops:
  0.0 35.0 %hyena_block.1 = bf16[32,32,256]{2,1,0:T(8,128)(2,1)} custom-call(s32[1,256]{1,0:T(1,128)} %ids_ref.1, bf16[512,2048]{1,0:T(8,128)(2,1)} %table_ref.1, f32[1,8192]{1,0:T(1,128)} %bitcast.9, bf16[3,2048,1024]{2,1,0:T(8,128)(2,1)} %bitcast.7, f32[3,3,1024]{2,1,0:T(4,128)} %taps_ref.1, f32[16,1024]{1,0:T(8,128)} %poles_ref.1, f32[16,1024]{1,0:T(8,128)} %res_ref.1, ...), custom_call_target="tpu_custom_call" | custom-call | tf_op jit(solution)/shard_map/hyena_block/pallas_call | solution.py:441
  35.0 2.0 %copy.9 = bf16[1024,256]{0,1:T(8,128)(2,1)} copy(bf16[1024,256]{1,0:T(8,128)(2,1)} %bitcast.8) | data formatting | bytes 1048576 | tf_op jit(solution)/shard_map/reshape | solution.py:501

commit v4 on v3

--- a/solution.py
+++ b/solution.py
@@ -34,6 +34,7 @@
 )
 
 
+BATCH = 8
 FAR_X = (2, 1, 3, 0)
 
 
@@ -403,9 +404,7 @@
             send_sem=out_send.at[part], recv_sem=out_recv, device_id=device, device_id_type=MESH,
         )
 
-    def gate(part, other):
-        s = lax.rem(other, FSDP)
-        j = lax.div(other, FSDP)
+    def gate(part, other, j, s):
         at = pl.ds(pl.multiple_of((s * CTX + j) * SUB, SUB), SUB)
         for half in range(2):
             q, u, c = [
@@ -420,10 +419,13 @@
         featurize(2 * part + 1)
         convolve(2 * part)
         convolve(2 * part + 1)
-        for other, device in others:
-            gate(part, other)
-            out_to(part, other, device).start()
-        gate(part, me)
+        for first in range(0, len(others), BATCH):
+            batch = others[first : first + BATCH]
+            for other, device in batch:
+                gate(part, other, device[0], device[1])
+            for other, device in batch:
+                out_to(part, other, device).start()
+        gate(part, me, i, y)
         pltpu.make_async_copy(pieces.at[me, share(part), :], out_ref.at[me, share(part), :], out_recv).start()
 
     sent = send_buf.at[pl.ds(0, GROUP - 1)]

time: 37.3 us -> 37.3 us (level)
  no operation moved by 1% of the time
where the time goes in v4:
time: 37.3 us; the launch traced here: 37.1 us
  Pallas kernels  35 us (94%)
  local copies, waits for them, and re-layouts  2.04 us (5%)
    pallas_call x1, Pallas kernels, block(): pl.pallas_call(block_kernel, out_shape=jax.ShapeDtypeStruct((GROUP, SLICE...  35 us
    reshape x1, local copies, waits for them, and re-layouts, shards(): return landed.reshape(CHAN, STEPS).T[None]  2.04 us

profile of v4, /device:TPU:1, one launch (start us, length us, event | category | flops | bytes accessed | tf_op | source)
XLA Modules:
  0.0 37.1 jit_solution(13443979024182803053)
XLA Ops:
  0.0 35.0 %hyena_block.1 = bf16[32,32,256]{2,1,0:T(8,128)(2,1)} custom-call(s32[1,256]{1,0:T(1,128)} %ids_ref.1, bf16[512,2048]{1,0:T(8,128)(2,1)} %table_ref.1, f32[1,8192]{1,0:T(1,128)} %bitcast.9, bf16[3,2048,1024]{2,1,0:T(8,128)(2,1)} %bitcast.7, f32[3,3,1024]{2,1,0:T(4,128)} %taps_ref.1, f32[16,1024]{1,0:T(8,128)} %poles_ref.1, f32[16,1024]{1,0:T(8,128)} %res_ref.1, ...), custom_call_target="tpu_custom_call" | custom-call | tf_op jit(solution)/shard_map/hyena_block/pallas_call | solution.py:443
  35.0 2.0 %copy.9 = bf16[1024,256]{0,1:T(8,128)(2,1)} copy(bf16[1024,256]{1,0:T(8,128)(2,1)} %bitcast.8) | data formatting | bytes 1048576 | tf_op jit(solution)/shard_map/reshape | solution.py:503
